TPU v7x, 512 devices: a whole 4x8x8 slice. The times are simulated.
512 devices in a mesh: fsdp: 16 (over x, z_hi, core), tok: 32 (over z_lo, y).
Axes of the slice: x: 4, y: 8, z: 8 (z_hi: 2, z_lo: 4; z = z_hi * 4 + z_lo), core: 2. Of those that a mesh axis runs over, the one named last changes fastest.
Arguments:
- queries: bfloat16 [16, 4096, 3072], P('fsdp', 'tok'), may hold values from -6 to 6
- keys: bfloat16 [16, 4096, 3072], P('fsdp', 'tok'), may hold values from -6 to 6
- values: bfloat16 [16, 4096, 3072], P('fsdp', 'tok'), may hold values from -6 to 6
- readout: bfloat16 [3072, 1000], P('fsdp'), may hold values from -12 to 12
- global_block: int32 [16], P('fsdp'), may hold values from 0 to 31
- q_gain: float32 [3072], replicated, may hold values from 0.5 to 5
- k_gain: float32 [3072], replicated, may hold values from 0.5 to 5
Outputs:
- entropy: float32 [], replicated
- q_grad: float32 [3072], replicated
- k_grad: float32 [3072], replicated
All inputs are finite; a program needn't handle non-finite values.
Results may differ from a plain program's by a relative error of at most 0.02.
The roundings to bfloat16 on the way count: a program that leaves them out, or rounds other values in their place, can miss the bound.
Values may be sent and summed in bfloat16 or wider, within the bound.
A program may use at most 64 MiB of HBM per device.

v0:
```python
import jax
import jax.numpy as jnp
from jax import lax
from jax.sharding import PartitionSpec as P

HEAD = 128
ROW = 64
GBLK = 128


score_entries = 1 << 20


def with_halo(x, sides, width):
    for axis, dim in sides:
        peers, length = (lax.axis_size(axis), x.shape[dim])
        up = [(i, (i + 1) % peers) for i in range(peers - 1)]
        down = [(j, i) for i, j in up]
        last = lax.slice_in_dim(x, length - width, length, axis=dim)
        first = lax.slice_in_dim(x, 0, width, axis=dim)
        before = lax.ppermute(last, axis, up)
        after = lax.ppermute(first, axis, down)
        x = jnp.concatenate([before, x, after], axis=dim)
    return x


def broadcast(block, axis, holder):
    block = jnp.where(lax.axis_index(axis) == holder, block, jnp.zeros_like(block))
    return lax.psum(block, axis)


def normalize(entries, gain):
    entries = entries.astype(jnp.float32)
    average = jnp.mean(entries, -1, keepdims=True)
    centred = entries - average
    variance = jnp.mean(centred * centred, -1, keepdims=True)
    return (centred * lax.rsqrt(variance + 1e-06) * gain).astype(jnp.bfloat16)


def group_total(query_part, key_part, value_part, usable, gain_query, gain_key):
    query_norm = normalize(query_part, gain_query)
    key_norm = normalize(key_part, gain_key)
    scores = jnp.einsum(
        "qhd,khd->hqk", query_norm, key_norm, preferred_element_type=jnp.float32
    ) * HEAD ** (-0.5)
    scores = jnp.where(usable[None, None, :], scores, -1e30)
    row_max = jnp.max(scores, -1, keepdims=True)
    exponent = jnp.exp(scores - row_max)
    row_total = jnp.sum(exponent, -1, keepdims=True)
    attention = (exponent / row_total).astype(jnp.bfloat16)
    return jnp.einsum("hqk,khd->hd", attention, value_part, preferred_element_type=jnp.float32)


def pick_group(head_count, row_count, key_count):
    chosen_size = 1
    for candidate in range(1, head_count + 1):
        if head_count % candidate == 0 and candidate * row_count * key_count <= score_entries:
            chosen_size = candidate
    return chosen_size


def attend_sum(query_rows, context, usable, gain_query, gain_key, group_size):
    head_count = gain_query.shape[0] // HEAD
    query_heads = query_rows.reshape(query_rows.shape[0], head_count, HEAD)
    key_heads = context[0].reshape(context.shape[1], head_count, HEAD)
    value_heads = context[1].reshape(context.shape[1], head_count, HEAD)
    query_gains = gain_query.reshape(head_count, HEAD)
    key_gains = gain_key.reshape(head_count, HEAD)
    checked = jax.checkpoint(group_total)

    def per_group(group_index):
        first_head = group_index * group_size
        return checked(
            lax.dynamic_slice_in_dim(query_heads, first_head, group_size, 1),
            lax.dynamic_slice_in_dim(key_heads, first_head, group_size, 1),
            lax.dynamic_slice_in_dim(value_heads, first_head, group_size, 1),
            usable,
            lax.dynamic_slice_in_dim(query_gains, first_head, group_size, 0),
            lax.dynamic_slice_in_dim(key_gains, first_head, group_size, 0),
        )

    return lax.map(per_group, jnp.arange(head_count // group_size, dtype=jnp.int32)).reshape(-1)


def body(queries, keys, values, readout, global_block, q_gain, k_gain):
    tok_count = lax.axis_size("tok")
    view_count = lax.axis_size("fsdp")
    position = lax.axis_index("tok")
    query_rows = queries[0]
    tok_dev = query_rows.shape[0]
    view_tokens = tok_dev * tok_count
    key_value = jnp.stack([keys[0], values[0]])
    padded = with_halo(key_value, (("tok", 1),), ROW)
    lower_rows = padded[:, :ROW]
    upper_rows = padded[:, ROW + tok_dev :]
    global_id = global_block[0]
    per_device = tok_dev // GBLK
    owner_index = global_id // per_device
    shared = broadcast(key_value, "tok", owner_index)
    context = jnp.concatenate([key_value, lower_rows, upper_rows, shared], axis=1)
    usable = jnp.concatenate(
        [
            jnp.ones((tok_dev,), bool),
            jnp.full((ROW,), position > 0),
            jnp.full((ROW,), position < tok_count - 1),
            jnp.ones((GBLK,), bool),
        ]
    )
    group_size = pick_group(q_gain.shape[0] // HEAD, tok_dev, context.shape[1])

    def local_total(gain_query, gain_key):
        return attend_sum(query_rows, context, usable, gain_query, gain_key, group_size)

    band_total, pullback = jax.vjp(local_total, q_gain, k_gain)
    pooled = lax.psum(band_total, "tok") / view_tokens
    weight = lax.all_gather(readout, "fsdp", axis=0, tiled=True).astype(jnp.float32)
    logits = jnp.dot(pooled, weight, precision=lax.Precision.HIGHEST)
    view_probs = jax.nn.softmax(logits, -1)
    mean_probs = lax.psum(view_probs, "fsdp") / view_count
    entropy = -jnp.sum(mean_probs * jnp.log(mean_probs))
    upstream = -(jnp.log(mean_probs) + 1.0) / view_count
    dlogits = view_probs * (upstream - jnp.sum(view_probs * upstream))
    dpooled = jnp.dot(weight, dlogits, precision=lax.Precision.HIGHEST)
    query_grad, key_grad = pullback(dpooled / view_tokens)
    query_grad, key_grad = lax.psum((query_grad, key_grad), ("fsdp", "tok"))
    return (entropy, query_grad, key_grad)


def solution(mesh):
    in_specs = (
        P("fsdp", "tok", None),
        P("fsdp", "tok", None),
        P("fsdp", "tok", None),
        P("fsdp", None),
        P("fsdp"),
        P(),
        P(),
    )
    out_specs = (P(), P(), P())
    return jax.shard_map(body, mesh=mesh, in_specs=in_specs, out_specs=out_specs, check_vma=False)
```

profile of v0, /device:TPU:1, one launch (start us, length us, event | category | flops | bytes accessed | tf_op | source)
XLA Modules:
  0.0 733.5 jit_solution(5594586090771126029)
XLA Ops:
  8.0 1.5 copy.22
  9.6 1.5 copy.23
  11.7 1.3 fusion.91
  13.6 1.7 fusion.89
  15.3 2.4 copy.24
  17.8 4.9 collective-permute-start
  22.7 1.4 copy.25
  24.1 1.3 collective-permute-start.1
  25.5 2.4 copy.21
  27.9 7.7 %collective-permute-done = bf16[2,64,3072]{2,1,0:T(8,128)(2,1)} collective-permute-done((bf16[2,64,3072]{2,1,0:T(8,128)(2,1)}, bf16[2,64,3072]{2,1,0:T(8,128)(2,1)}, u32[]{:S(2)}, u32[]{:S(2)}) %collective-permute-start) | collective-permute-done | bytes 786464 | tf_op jit(solution)/shard_map/ppermute | solution.py:21
  35.6 1.8 copy.26
  37.4 4.9 collective-permute-done.1
  42.2 2.5 copy.27
  44.7 265.8 %all-reduce.3.cloned.1.call-done = bf16[2,128,3072]{1,2,0:T(8,128)(2,1)} async-done(((bf16[2,128,3072]{1,2,0:T(8,128)(2,1)}), bf16[2,128,3072]{1,2,0:T(8,128)(2,1)}) %all-reduce.3.cloned.1.call-update) | async-done | bytes 1572880 | tf_op jit(solution)/shard_map/psum | solution.py:29
  310.5 3.8 pad_maximum_fusion
  314.4 2.7 fusion.98
  317.1 34.2 %while.44 = (s32[]{:T(128)}, f32[2,12,128]{2,1,0:T(8,128)}, s32[2]{0:T(128)}, bf16[2,128,12,128]{3,1,2,0:T(8,128)(2,1)}, bf16[2,384,12,128]{3,1,2,0:T(8,128)(2,1...) while((s32[]{:T(128)}, f32[2,12,128]{2,1,0:T(8,128)}, ...), condition=%wide.region_9.10_spmd.clone, body=%wide.region_1.9_spmd.clone.sunk | while | flops 164959488 | bytes 33304724 | solution.py:82
  318.3 1.9 constant_dynamic-slice_fusion.9
  321.5 1.4 fusion.145
  324.0 2.6 convert_reduce_fusion.17
  328.3 2.0 copy.68
  330.3 2.8 bitcast_dynamic-update-slice_fusion.15
  335.4 1.9 constant_dynamic-slice_fusion.9
  338.5 1.4 fusion.145
  341.0 2.6 convert_reduce_fusion.17
  345.3 2.0 copy.68
  347.4 2.9 bitcast_dynamic-update-slice_fusion.15
  352.0 122.8 %psum.36 = f32[3072]{0:T(1024)S(1)} all-reduce(f32[3072]{0:T(1024)S(1)} %reshape.126), channel_id=1, replica_groups=mesh['fsdp'=16,'tok'=32] {'tok'}, use_global_device_ids=true, to_apply=%region_10.11 | all-reduce | flops 3072 | bytes 24576 | tf_op jit(solution)/shard_map/psum | solution.py:115
  474.8 4.6 fusion.103
  481.2 1.3 fusion.95
  482.5 93.4 %psum.37 = f32[1000]{0:T(1024)S(1)} all-reduce(f32[1000]{0:T(1024)S(1)} %fusion.95), channel_id=1, replica_groups=mesh['fsdp'=16,'tok'=32] {'fsdp'}, use_global_device_ids=true, to_apply=%region_13.14 | all-reduce | flops 1000 | bytes 8000 | tf_op jit(solution)/shard_map/psum | solution.py:119
  575.9 1.9 multiply_reduce_fusion.1
  577.8 1.8 subtract_multiply_fusion
  579.7 7.9 %fusion.104 = f32[1,3072]{1,0:T(1,128)S(1)} fusion(f32[1000,1]{0,1:T(1,128)S(1)} %bitcast.116, bf16[3072,1000]{1,0:T(8,128)(2,1)} %all-gather.2.cloned.1.call-done), kind=kOutput, calls=%fused_computation.141 | convolution fusion | flops 36864000 | bytes 6160288 | tf_op jit(solution)/shard_map/dot_general | solution.py:123
  587.7 42.7 %while.43 = (s32[]{:T(128)}, f32[24,128]{1,0:T(8,128)S(1)}, f32[24,128]{1,0:T(8,128)S(1)}, s32[2]{0:T(128)S(1)}, bf16[2,128,12,128]{3,1,2,0:T(8,128)(2,1)}, /*in...) while((s32[]{:T(128)}, f32[24,128]{1,0:T(8,128)S(1)}, ...), condition=%wide.region_28.29_spmd, body=%wide.region_16.28_spmd.sunk | while | flops 497625600 | bytes 43781616 | solution.py:82
  588.0 1.4 copy-done.1
  591.3 1.4 fusion.133
  592.8 2.0 fusion.135
  596.7 1.7 convert_reduce_fusion.14
  598.5 3.7 fusion.140
  602.2 3.9 fusion.139
  609.4 1.4 copy-done.1
  612.7 1.4 fusion.133
  614.1 2.0 fusion.135
  618.0 1.7 convert_reduce_fusion.14
  619.8 3.7 fusion.140
  623.6 3.9 fusion.139
  631.0 93.9 %all-reduce = (f32[3072]{0:T(1024)}, f32[3072]{0:T(1024)}) all-reduce(f32[3072]{0:T(1024)S(1)} %bitcast.105, f32[3072]{0:T(1024)S(1)} %bitcast.106), channel_id=1, replica_groups=mesh['fsdp'=16,'tok'=32] {'fsdp','tok'}, use_global_device_ids=true, to_apply=%region_29.30 | all-reduce | flops 6144 | bytes 49152 | tf_op jit(solution)/shard_map/psum | solution.py:125
  (179 shorter events, 28.0 us)
Async XLA Ops:
  8.0 302.5 %all-reduce.3.cloned.1.call-start = ((), (), s32[]{:S(2)}) async-start(), calls=%async_computation | async-start | bytes 3145728 | tf_op jit(solution)/shard_map/psum | solution.py:29
  13.1 461.7 %all-gather.2.cloned.1.call-start = ((), (), s32[]{:S(2)}) async-start(), calls=%async_computation.1 | async-start | bytes 6684672 | tf_op jit(solution)/shard_map/all_gather | solution.py:116
  17.8 17.8 %collective-permute-start = (bf16[2,64,3072]{2,1,0:T(8,128)(2,1)}, bf16[2,64,3072]{2,1,0:T(8,128)(2,1)}, u32[]{:S(2)}, u32[]{:S(2)}) collective-permute-start(bf16[2,64,3072]{2,1,0:T(8,128)(2,1)} %copy.24), channel_id=1, source_target_pairs={{0,1},{1,2},{2,3},{3,4},{4,5},{5,6},{6,7},{7,8},{8,9},{9,10},{10,1... | collective-permute-start | bytes 2359304 | tf_op jit(solution)/shard_map/ppermute | solution.py:21
  24.1 18.1 %collective-permute-start.1 = (bf16[2,64,3072]{2,1,0:T(8,128)(2,1)}, bf16[2,64,3072]{2,1,0:T(8,128)(2,1)}, u32[]{:S(2)}, u32[]{:S(2)}) collective-permute-start(bf16[2,64,3072]{2,1,0:T(8,128)(2,1)} %copy.25), channel_id=1, source_target_pairs={{1,0},{2,1},{3,2},{4,3},{5,4},{6,5},{7,6},{8,7},{9,8},{10,9},{11,1... | collective-permute-start | bytes 2359304 | tf_op jit(solution)/shard_map/ppermute | solution.py:22
  314.4 2.7 copy-start.6
  317.1 1.2 copy-start.16
  321.0 1.9 copy-start.2
  321.0 2.9 copy-start.7
  321.0 2.9 copy-start.8
  321.1 2.9 copy-start.11
  324.0 2.6 copy-start.9
  324.0 2.6 copy-start.12
  324.0 3.1 copy-start.14
  327.1 3.2 copy-start.15
  328.3 4.9 copy-start.3
  330.3 2.9 copy-start.18
  330.3 3.8 copy-start.17
  333.2 0.9 copy-start.4
  333.3 0.8 copy-start.19
  334.1 1.2 copy-start.16
  338.1 1.9 copy-start.2
  338.1 2.9 copy-start.7
  338.1 2.9 copy-start.8
  338.1 2.9 copy-start.11
  341.0 2.6 copy-start.9
  341.0 2.6 copy-start.12
  341.0 3.1 copy-start.14
  344.2 3.2 copy-start.15
  345.3 5.0 copy-start.3
  347.4 3.0 copy-start.18
  347.4 3.9 copy-start.17
  350.4 0.9 copy-start.4
  350.5 0.8 copy-start.19
  579.7 8.0 %copy-start = (bf16[2,384,12,128]{3,2,1,0:T(8,128)(2,1)S(1)}, bf16[2,384,12,128]{3,2,1,0:T(8,128)(2,1)}, u32[]{:S(2)}) copy-start(bf16[2,384,12,128]{3,2,1,0:T(8,128)(2,1)} %get-tuple-element.851) | copy-start | bytes 7077892
  579.7 8.0 %copy-start.10 = (f32[2,12,128]{2,1,0:T(8,128)S(1)}, f32[2,12,128]{2,1,0:T(8,128)}, u32[]{:S(2)}) copy-start(f32[2,12,128]{2,1,0:T(8,128)} %get-tuple-element.852) | copy-start | bytes 36868
  579.7 8.0 %copy-start.13 = (f32[2,12,128]{2,1,0:T(8,128)S(1)}, f32[2,12,128]{2,1,0:T(8,128)}, u32[]{:S(2)}) copy-start(f32[2,12,128]{2,1,0:T(8,128)} %get-tuple-element.853) | copy-start | bytes 36868
  579.7 8.0 %copy-start.20 = (s32[2]{0:T(128)S(1)}, s32[2]{0:T(128)}, u32[]{:S(2)}) copy-start(s32[2]{0:T(128)} %get-tuple-element.848) | copy-start | bytes 28
  587.7 1.7 copy-start.1
  587.7 1.8 copy-start.5
  609.0 1.7 copy-start.1
  609.1 1.8 copy-start.5
Sparse Core Ops, SparseCore 0:
  13.2 297.2 all-reduce.2
Sparse Core Ops, SparseCore 1:
  17.3 122.0 all-gather.1
where the time goes:
time: 734 us; the launch traced here: 733 us
  blocking collectives  310 us (42%)
  waiting for transfers between devices  279 us (38%)
  local copies, waits for them, and re-layouts  46.3 us (6%)
  matrix products  39.1 us (5%)
  other arithmetic  32.6 us (4%)
  between operations  18.1 us (2%)
    psum x1, waiting for transfers between devices, broadcast(): return lax.psum(block, axis)  266 us
    psum x1, blocking collectives, body(): pooled = lax.psum(band_total, 'tok') / view_tokens  123 us
    psum x1, blocking collectives, body(): query_grad, key_grad = lax.psum((query_grad, key_grad), ('fsdp', 'tok'))  93.9 us
    psum x1, blocking collectives, body(): mean_probs = lax.psum(view_probs, 'fsdp') / view_count  93.4 us
    dot_general x6, matrix products, group_total(): jnp.einsum('qhd,khd->hqk', query_norm, key_norm, preferred_element_type=j...  19.3 us
  transfers between devices with their start and end apart: 4, of which 3 were waited for; matrix products, arithmetic and copies ran while one was open for 7% of the time, Pallas kernels for 0%

commit v1 on v0

v1 whole, which is shorter than its diff:
```python
import functools

import jax
import jax.numpy as jnp
from jax import lax
from jax.experimental import pallas as pl
from jax.experimental.pallas import tpu as pltpu
from jax.sharding import PartitionSpec as P

HEAD = 128
ROW = 64
BAND = 128
CLASSES = 1000
PAD = 1024
WIN = BAND + 2 * ROW
SEEN = WIN + BAND
Y = 8
MESH = pl.DeviceIdType.MESH
F32 = jnp.float32
BF16 = jnp.bfloat16
NT = (((1,), (1,)), ((), ()))
NN = (((1,), (0,)), ((), ()))
TN = (((0,), (0,)), ((), ()))
SCALE = HEAD**-0.5


def dot(a, b, dims):
    return lax.dot_general(a, b, dims, preferred_element_type=F32)


def normalize(x, gain):
    x = x.astype(F32)
    x = x - jnp.mean(x, -1, keepdims=True)
    var = jnp.mean(x * x, -1, keepdims=True)
    return (x * lax.rsqrt(var + 1e-06) * gain).astype(BF16)


def split3(x):
    x = jnp.broadcast_to(x, (16, x.shape[1]))
    high = x.astype(BF16).astype(F32)
    rest = x - high
    mid = rest.astype(BF16).astype(F32)
    low = rest - mid
    row = lax.broadcasted_iota(jnp.int32, x.shape, 0)
    out = jnp.where(row == 0, high, jnp.where(row == 1, mid, jnp.where(row == 2, low, 0.0)))
    return out.astype(BF16)


def row_dot(x, b, dims):
    return jnp.sum(dot(split3(x), b, dims), 0, keepdims=True)


def kernel(
    ny, nz, nf, hc, tokens,
    gid_ref, q_ref, k_ref, v_ref, r_ref, qg_ref, kg_ref,
    ent_ref, w_out,
    kpad, vpad, qbuf, knpad, kng, zk, zv, rraw, rpad, att, qn_s, w_s, e_acc, eg_acc, e_bf, eg_bf,
    lbuf, pbuf, wbuf, tbuf,
    ks, kr, vs, vr, qs, qr, local, zks, zkr, zvs, zvr, hks, hkr, hvs, hvr,
    rs, rr, fs, fr, lsem, lrem, psem, prem, wsem, wrem, tsem, trem,
):
    nt = nz * ny
    f, t = lax.axis_index("fsdp"), lax.axis_index("tok")
    z, y = t // ny, t % ny
    core = f % 2
    width = hc * HEAD
    rows = ny * BAND
    shard = r_ref.shape[0]

    def copy(src, dst, ssem, rsem, dev):
        return pltpu.make_async_remote_copy(
            src_ref=src, dst_ref=dst, send_sem=ssem, recv_sem=rsem, device_id=dev, device_id_type=MESH
        )

    def chunk(c):
        return pl.ds(pl.multiple_of(c * width, HEAD), width)

    def band_rows(b):
        return pl.ds(pl.multiple_of(ROW + b * BAND, ROW), BAND)

    own_k = pltpu.make_async_copy(k_ref.at[0, :, chunk(y)], kpad.at[band_rows(y)], local.at[0])
    own_v = pltpu.make_async_copy(v_ref.at[0, :, chunk(y)], vpad.at[band_rows(y)], local.at[1])
    own_q = pltpu.make_async_copy(q_ref.at[0, :, chunk(y)], qbuf.at[y], local.at[2])
    own_k.start()
    own_v.start()
    own_q.start()

    barrier = pltpu.get_barrier_semaphore()

    def greet_t(d, carry):
        pl.semaphore_signal(barrier, inc=1, device_id=(f, (t + d) % nt), device_id_type=MESH)
        return carry

    def greet_f(d, carry):
        pl.semaphore_signal(barrier, inc=1, device_id=((f + d) % nf, t), device_id_type=MESH)
        return carry

    lax.fori_loop(1, nt, greet_t, 0)
    lax.fori_loop(1, nf, greet_f, 0)
    pl.semaphore_wait(barrier, nt - 1 + nf - 1)

    order = [0]
    for d in range(1, ny // 2 + 1):
        order.append(d)
        if ny - d != d:
            order.append(ny - d)

    def y_dev(d):
        return (f, z * ny + (y + d) % ny)

    def k_copy(d):
        p = (y + d) % ny
        return copy(k_ref.at[0, :, chunk(p)], kpad.at[band_rows(y)], ks.at[d], kr.at[d], y_dev(d))

    def v_copy(d):
        p = (y + d) % ny
        return copy(v_ref.at[0, :, chunk(p)], vpad.at[band_rows(y)], vs.at[d], vr.at[d], y_dev(d))

    def q_copy(d):
        p = (y + d) % ny
        return copy(q_ref.at[0, :, chunk(p)], qbuf.at[y], qs.at[d], qr.at[d], y_dev(d))

    far_first = order[:0:-1]
    for d in far_first:
        k_copy(d).start()

    mine = pl.ds(pl.multiple_of(core * shard, 64), shard)
    has_rows = f // 2 == y

    def r_copy(d):
        return copy(r_ref, rraw.at[mine], rs.at[d], rr.at[0], ((f + 2 * d) % nf, t))

    def r_local():
        return pltpu.make_async_copy(r_ref, rraw.at[mine], local.at[3])

    @pl.when(has_rows)
    def _():
        for d in range(1, nf // 2):
            r_copy(d).start()
        r_local().start()

    for d in far_first:
        k_copy(d).wait_send()
    for d in far_first:
        v_copy(d).start()

    own_k.wait()
    for d in far_first:
        k_copy(d).wait_recv()
    gid = gid_ref[0]
    gid_y, gid_z = lax.rem(gid, ny), lax.div(gid, ny)

    def pick(parts, want):
        out = None
        for i, part in enumerate(parts):
            part = part.astype(F32) * jnp.where(want == i, 1.0, 0.0)
            out = part if out is None else out + part
        return out.astype(BF16)

    def pick_row(pad):
        return pick([pad[ROW + b * BAND : ROW + (b + 1) * BAND, :] for b in range(ny)], gid_y)

    def z_dev(d):
        return (f, ((z + d) % nz) * ny + y)

    def z_copy(buf, ssem, rsem, d):
        return copy(buf.at[z], buf.at[z], ssem.at[d], rsem.at[d], z_dev(d))

    def end_copies(pad, ssem, rsem):
        up = copy(pad.at[pl.ds(rows, ROW)], pad.at[pl.ds(0, ROW)], ssem.at[0], rsem.at[0], z_dev(1))
        down = copy(pad.at[pl.ds(ROW, ROW)], pad.at[pl.ds(ROW + rows, ROW)], ssem.at[1], rsem.at[1], z_dev(nz - 1))
        return up, down

    zk[z] = pick_row(kpad)
    for d in range(1, nz):
        z_copy(zk, zks, zkr, d).start()
    for c in end_copies(kpad, hks, hkr):
        c.start()

    q_gain = [qg_ref[pl.ds(y * hc + h, 1), :] for h in range(hc)]
    k_gain = [kg_ref[pl.ds(y * hc + h, 1), :] for h in range(hc)]
    knpad[:, :, HEAD:] = jnp.ones((hc, rows + 2 * ROW, HEAD), BF16)
    kng[:, :, HEAD:] = jnp.ones((hc, BAND, HEAD), BF16)

    def norm_rows(at, size):
        for h in range(hc):
            knpad[h, at, :HEAD] = normalize(kpad[at, h * HEAD : (h + 1) * HEAD], k_gain[h])

    def norm_band(b, carry):
        norm_rows(band_rows(b), BAND)
        return carry

    lax.fori_loop(0, ny, norm_band, 0)

    for d in far_first:
        v_copy(d).wait_send()
    for d in far_first:
        q_copy(d).start()

    for d in range(1, nz):
        z_copy(zk, zks, zkr, d).wait_recv()
    for c in end_copies(kpad, hks, hkr):
        c.wait_recv()
    norm_rows(pl.ds(0, ROW), ROW)
    norm_rows(pl.ds(ROW + rows, ROW), ROW)
    kg_raw = pick([zk[i] for i in range(nz)], gid_z)
    for h in range(hc):
        kng[h, :, :HEAD] = normalize(kg_raw[:, h * HEAD : (h + 1) * HEAD], k_gain[h])

    own_v.wait()
    for d in far_first:
        v_copy(d).wait_recv()
    zv[z] = pick_row(vpad)
    for d in range(1, nz):
        z_copy(zv, zvs, zvr, d).start()
    for c in end_copies(vpad, hvs, hvr):
        c.start()

    @pl.when(has_rows)
    def _():
        r_local().wait()

    @pl.when(jnp.logical_not(has_rows))
    def _():
        r_copy(1).wait_recv()

    def twin_copy(at):
        return copy(rraw.at[at], rraw.at[at], fs, fr, (f + 1 - 2 * core, t))

    twin_copy(mine).start()

    ones16 = jnp.ones((16, BAND), BF16)
    lane = lax.broadcasted_iota(jnp.int32, (BAND, WIN), 1)

    def band(b):
        low = jnp.where((z == 0) & (b == 0), ROW, 0)
        high = jnp.where((z == nz - 1) & (b == ny - 1), ROW + BAND, WIN)
        usable = (lane >= low) & (lane < high)
        window = pl.ds(pl.multiple_of(b * BAND, BAND), WIN)
        for h in range(hc):
            qn = normalize(qbuf[b, :, h * HEAD : (h + 1) * HEAD], q_gain[h])
            qn_s[b, h] = qn
            near = dot(qn, knpad[h, window, :HEAD], NT) * SCALE
            far = dot(qn, kng[h, :, :HEAD], NT) * SCALE
            near = jnp.where(usable, near, -1e30)
            top = jnp.maximum(jnp.max(near, -1, keepdims=True), jnp.max(far, -1, keepdims=True))
            near = jnp.exp(near - top)
            far = jnp.exp(far - top)
            total = jnp.sum(near, -1, keepdims=True) + jnp.sum(far, -1, keepdims=True)
            inv = 1.0 / total
            near = (near * inv).astype(BF16)
            far = (far * inv).astype(BF16)
            att[b, h, :, :WIN] = near
            att[b, h, :, WIN:] = far
            w_s[b, h, :, :WIN] = dot(ones16, near, NN)[:8]
            w_s[b, h, :, WIN:] = dot(ones16, far, NN)[:8]

    own_q.wait()
    for d in order:
        if d:
            q_copy(ny - d).wait_recv()
        band((y + d) % ny)

    for d in range(1, nz):
        z_copy(zv, zvs, zvr, d).wait_recv()
    for c in end_copies(vpad, hvs, hvr):
        c.wait_recv()
    other = pl.ds(pl.multiple_of((1 - core) * shard, 64), shard)
    twin_copy(other).wait_recv()
    rpad[:, CLASSES // HEAD * HEAD :] = jnp.zeros((width, PAD - CLASSES // HEAD * HEAD), BF16)
    rpad[:, :CLASSES] = rraw[...]

    vg = pick([zv[i] for i in range(nz)], gid_z)
    pooled = []
    for h in range(hc):
        parts = [jnp.zeros((1, HEAD), F32) for _ in range(ny + 1)]
        far = jnp.zeros((1, HEAD), F32)
        for b in range(ny):
            parts[b] = parts[b] + w_s[b, h, 0:1, :HEAD]
            parts[b + 1] = parts[b + 1] + w_s[b, h, 0:1, HEAD:WIN]
            far = far + w_s[b, h, 0:1, WIN:]
        cols = slice(h * HEAD, (h + 1) * HEAD)
        pooled.append(row_dot(jnp.concatenate(parts, 1), vpad[:, cols], NN) + row_dot(far, vg[:, cols], NN))
    pooled = jnp.concatenate(pooled, 1) * (1.0 / tokens)
    logits = row_dot(pooled, rpad[...], NN)
    for i in range(8):
        lbuf[t, i : i + 1, :] = logits[:, i * HEAD : (i + 1) * HEAD]

    def exchange(buf, n, me, dev, ssem, rsem):
        def one(d):
            return copy(buf.at[me], buf.at[me], ssem.at[d], rsem.at[d], dev((me + d) % n))

        def start():
            def step(d, carry):
                one(d).start()
                return carry

            lax.fori_loop(1, n, step, 0)

        def wait():
            def step(d, carry):
                one(d).wait_recv()
                return carry

            lax.fori_loop(1, n, step, 0)

        def wait_sent():
            def step(d, carry):
                one(d).wait_send()
                return carry

            lax.fori_loop(1, n, step, 0)

        return start, wait, wait_sent

    def t_dev(p):
        return (f, p)

    def f_dev(p):
        return (p, t)

    def total_of(buf, n):
        out = buf[0]
        for i in range(1, n):
            out = out + buf[i]
        return out

    l_start, l_wait, l_sent = exchange(lbuf, nt, t, t_dev, lsem, lrem)
    p_start, p_wait, p_sent = exchange(pbuf, nf, f, f_dev, psem, prem)
    w_start, w_wait, w_sent = exchange(wbuf, nf, f, f_dev, wsem, wrem)
    t_start, t_wait, t_sent = exchange(tbuf, nt, t, t_dev, tsem, trem)
    l_start()

    e_acc[...] = jnp.zeros_like(e_acc)
    eg_acc[...] = jnp.zeros_like(eg_acc)

    def pulled(b, carry):
        window = pl.ds(pl.multiple_of(b * BAND, BAND), WIN)
        for h in range(hc):
            near = att[b, h, :, :WIN]
            far = att[b, h, :, WIN:]
            kn = knpad[h, window, :]
            kg = kng[h]
            mean_key = dot(near, kn, NN) + dot(far, kg, NN)
            qn = qn_s[b, h]
            qk = qn.astype(F32) * (mean_key[:, :HEAD] / mean_key[:, HEAD:])
            qk_high = qk.astype(BF16)
            qk_low = (qk - qk_high.astype(F32)).astype(BF16)
            right = jnp.concatenate([qn, qk_high, qk_low], 1)
            got = dot(near, right, TN)
            e_acc[h, window, :] += (
                kn[:, :HEAD].astype(F32) * got[:, :HEAD] - got[:, HEAD : 2 * HEAD] - got[:, 2 * HEAD :]
            )
            got = dot(far, right, TN)
            eg_acc[h] += kg[:, :HEAD].astype(F32) * got[:, :HEAD] - got[:, HEAD : 2 * HEAD] - got[:, 2 * HEAD :]
        return carry

    lax.fori_loop(0, ny // 2, pulled, 0)

    l_wait()
    logits = total_of(lbuf, nt)
    place = lax.broadcasted_iota(jnp.int32, (8, HEAD), 0) * HEAD + lax.broadcasted_iota(jnp.int32, (8, HEAD), 1)
    valid = place < CLASSES
    logits = jnp.where(valid, logits, -jnp.inf)

    def all_sum(x):
        return jnp.sum(jnp.sum(x, 0, keepdims=True), 1, keepdims=True)

    top = jnp.max(jnp.max(logits, 0, keepdims=True), 1, keepdims=True)
    probs = jnp.exp(logits - top)
    probs = probs / all_sum(probs)
    pbuf[f] = probs
    p_start()

    lax.fori_loop(ny // 2, ny, pulled, 0)
    e_bf[...] = e_acc[...].astype(BF16)
    eg_bf[...] = eg_acc[...].astype(BF16)

    p_wait()
    mean = total_of(pbuf, nf) * (1.0 / nf)
    log_mean = jnp.where(valid, jnp.log(mean), 0.0)
    entropy = -all_sum(jnp.where(valid, mean * log_mean, 0.0))
    ent_ref[...] = jnp.broadcast_to(entropy, ent_ref.shape)
    upstream = jnp.where(valid, -(log_mean + 1.0) * (1.0 / nf), 0.0)
    dlogits = probs * (upstream - all_sum(probs * upstream))
    dlogits = jnp.concatenate([dlogits[i : i + 1] for i in range(8)], 1)
    dpooled = row_dot(dlogits, rpad[...], NT) * (1.0 / tokens)
    wbuf[f] = jnp.zeros((8, HEAD), F32)
    for h in range(hc):
        cols = slice(h * HEAD, (h + 1) * HEAD)
        down = dpooled[:, cols]
        near = row_dot(down, vpad[:, cols], NT)
        far = row_dot(down, vg[:, cols], NT)
        middle = (jnp.sum(near, 1, keepdims=True) + jnp.sum(far, 1, keepdims=True)) * (1.0 / (rows + 2 * ROW + BAND))
        got = row_dot(near - middle, e_bf[h], NN) + row_dot(far - middle, eg_bf[h], NN)
        wbuf[f, h : h + 1, :] = got * SCALE
    w_start()
    w_wait()
    tbuf[t] = total_of(wbuf, nf)
    t_start()
    t_wait()
    for i in range(ny):
        got = tbuf[i]
        for j in range(1, nz):
            got = got + tbuf[j * ny + i]
        w_out[i * hc : (i + 1) * hc, :] = got[:hc]

    for d in far_first:
        q_copy(d).wait_send()
    for d in range(1, nz):
        z_copy(zk, zks, zkr, d).wait_send()
        z_copy(zv, zvs, zvr, d).wait_send()
    for c in end_copies(kpad, hks, hkr) + end_copies(vpad, hvs, hvr):
        c.wait_send()

    @pl.when(has_rows)
    def _():
        for d in range(1, nf // 2):
            r_copy(d).wait_send()

    twin_copy(mine).wait_send()
    l_sent()
    p_sent()
    w_sent()
    t_sent()


def make_body(ny):
    def body(queries, keys, values, readout, global_block, q_gain, k_gain):
        nf, nt = lax.axis_size("fsdp"), lax.axis_size("tok")
        nz = nt // ny
        heads = q_gain.shape[0] // HEAD
        hc = heads // ny
        width = hc * HEAD
        rows = ny * BAND
        padded = rows + 2 * ROW
        tokens = nt * BAND
        dma = pltpu.SemaphoreType.DMA
        vmem = pltpu.VMEM
        scratch = [
            vmem((padded, width), BF16),
            vmem((padded, width), BF16),
            vmem((ny, BAND, width), BF16),
            vmem((hc, padded, 2 * HEAD), BF16),
            vmem((hc, BAND, 2 * HEAD), BF16),
            vmem((nz, BAND, width), BF16),
            vmem((nz, BAND, width), BF16),
            vmem((width, CLASSES), BF16),
            vmem((width, PAD), BF16),
            vmem((ny, hc, BAND, SEEN), BF16),
            vmem((ny, hc, BAND, HEAD), BF16),
            vmem((ny, hc, 8, SEEN), F32),
            vmem((hc, padded, HEAD), F32),
            vmem((hc, BAND, HEAD), F32),
            vmem((hc, padded, HEAD), BF16),
            vmem((hc, BAND, HEAD), BF16),
            vmem((nt, 8, HEAD), F32),
            vmem((nf, 8, HEAD), F32),
            vmem((nf, 8, HEAD), F32),
            vmem((nt, 8, HEAD), F32),
        ]
        scratch += [dma((ny,))] * 6 + [dma((4,))] + [dma((nz,))] * 4 + [dma((2,))] * 4
        scratch += [dma((nf // 2,)), dma((1,)), dma, dma]
        scratch += [dma((nt,))] * 2 + [dma((nf,))] * 4 + [dma((nt,))] * 2
        hbm = pl.BlockSpec(memory_space=pl.ANY)
        whole = pl.BlockSpec(memory_space=pltpu.VMEM)
        entropy, total = pl.pallas_call(
            functools.partial(kernel, ny, nz, nf, hc, tokens),
            out_shape=(
                jax.ShapeDtypeStruct((8, HEAD), F32),
                jax.ShapeDtypeStruct((heads, HEAD), F32),
            ),
            in_specs=[pl.BlockSpec(memory_space=pltpu.SMEM), hbm, hbm, hbm, hbm, whole, whole],
            out_specs=(whole, whole),
            scratch_shapes=scratch,
            compiler_params=pltpu.CompilerParams(
                collective_id=0, has_side_effects=True, vmem_limit_bytes=60 * 2**20
            ),
            name="adapt",
        )(
            global_block,
            queries,
            keys,
            values,
            readout,
            q_gain.reshape(heads, HEAD),
            k_gain.reshape(heads, HEAD),
        )
        total = total.reshape(-1)
        return entropy[0, 0], total / q_gain, total / k_gain

    return body


def solution(mesh):
    in_specs = (
        P("fsdp", "tok", None),
        P("fsdp", "tok", None),
        P("fsdp", "tok", None),
        P("fsdp", None),
        P("fsdp"),
        P(),
        P(),
    )
    out_specs = (P(), P(), P())
    return jax.shard_map(make_body(Y), mesh=mesh, in_specs=in_specs, out_specs=out_specs, check_vma=False)
```

time: 734 us -> 144 us (0.20)
  blocking collectives: 310 us -> 0 us
  waiting for transfers between devices: 279 us -> 0 us
  Pallas kernels: 0 us -> 140 us
  local copies, waits for them, and re-layouts: 46.3 us -> 1.2 us
  matrix products: 39.1 us -> 0 us
  other arithmetic: 32.6 us -> 1.32 us
  between operations: 18.1 us -> 1.3 us
    psum x3 -> x0, blocking collectives: 310 us -> none  [the longest x1 123 us: body(): pooled = lax.psum(band_total, 'tok') / view_tokens]
    psum x1 -> x0, waiting for transfers between devices: 266 us -> none  [broadcast(): return lax.psum(block, axis)]
    pallas_call x0 -> x1, Pallas kernels: none -> 140 us  [body(): pl.pallas_call(functools.partial(kernel, ny, nz, nf, hc, tokens), out_sha...]
    dot_general x12 -> x0, matrix products: 33.9 us -> none  [the longest x6 19.3 us: group_total(): jnp.einsum('qhd,khd->hqk', query_norm, key_norm, preferred_element_type=j...]
    reduce_sum x24 -> x0, other arithmetic: 20.4 us -> none  [the longest x8 7.75 us: normalize(): variance = jnp.mean(centred * centred, -1, keepdims=True)]
    ppermute x2 -> x0, waiting for transfers between devices: 12.5 us -> none  [the longest x1 7.67 us: with_halo(): before = lax.ppermute(last, axis, up)]
    dynamic_slice x14 -> x0, local copies, waits for them, and re-layouts: 12.3 us -> none  [the longest x4 7.89 us: per_group(): lax.dynamic_slice_in_dim(value_heads, first_head, group_size, 1)]
    dynamic_update_slice x12 -> x0, local copies, waits for them, and re-layouts: 8.39 us -> none  [attend_sum(): lax.map(per_group, jnp.arange(head_count // group_size, dtype=jnp.int32))]
  transfers between devices with their start and end apart: 4 -> 0, of which waited for: 3 -> 0; matrix products, arithmetic and copies ran while one was open for 7% -> 0% of each run, Pallas kernels for 0% -> 0%
where the time goes in v1:
time: 144 us
  Pallas kernels  140 us (97%)
    pallas_call x1, Pallas kernels, body(): pl.pallas_call(functools.partial(kernel, ny, nz, nf, hc, tokens), out_sha...  140 us

profile of v1, /device:TPU:1, one launch (start us, length us, event | category | flops | bytes accessed | tf_op | source)
XLA Modules:
  0.0 144.0 jit_solution(14006671659576700786)
XLA Ops:
  1.3 0.0 copy-start
  1.3 0.0 copy-start.1
  1.3 140.2 %adapt.1 = (f32[8,128]{1,0:T(8,128)}, f32[24,128]{1,0:T(8,128)}) custom-call(s32[1]{0:T(128)S(6)} %copy.10.gid_ref, bf16[1,128,3072]{2,1,0:T(8,128)(2,1)} %q_ref.1, bf16[1,128,3072]{2,1,0:T(8,128)(2,1)} %k_ref.1, bf16[1,128,3072]{2,1,0:T(8,128)(2,1)} %v_ref.1, bf16[192,1000]{1,0:T(8,128)(2,1)} %r_ref.1, f32[24,128]{1,0:T(8,128)} %bitcast.6, f32[24,128]{1,0:T(8,128)} %bitcast.7), custom_call_target="tpu_custom_call" | custom-call | tf_op jit(solution)/shard_map/adapt/pallas_call | solution.py:467
  141.5 1.2 slice.3
  142.7 0.0 copy-done
  142.7 0.0 copy-done.1
  142.7 1.3 bitcast_divide_fusion
Async XLA Ops:
  1.3 141.4 %copy-start = (f32[3072]{0:T(1024)S(1)}, f32[3072]{0:T(1024)}, u32[]{:S(2)}) copy-start(f32[3072]{0:T(1024)} %param.12) | copy-start | bytes 36868
  1.3 141.4 %copy-start.1 = (f32[3072]{0:T(1024)S(1)}, f32[3072]{0:T(1024)}, u32[]{:S(2)}) copy-start(f32[3072]{0:T(1024)} %param.13) | copy-start | bytes 36868

commit v2 on v1

--- a/solution.py
+++ b/solution.py
@@ -52,11 +52,12 @@
 
 def kernel(
     ny, nz, nf, hc, tokens,
-    gid_ref, q_ref, k_ref, v_ref, r_ref, qg_ref, kg_ref,
+    gid_hbm, q_ref, k_ref, v_ref, r_ref, qg_hbm, kg_hbm,
     ent_ref, w_out,
-    kpad, vpad, qbuf, knpad, kng, zk, zv, rraw, rpad, att, qn_s, w_s, e_acc, eg_acc, e_bf, eg_bf,
+    gid_ref, qg_ref, kg_ref,
+    kpad, vbuf, vend, qbuf, knpad, kng, zk, zv, zw, rraw, rpad, att, qn_s, w_s, e_acc, eg_acc, e_bf, pull,
     lbuf, pbuf, wbuf, tbuf,
-    ks, kr, vs, vr, qs, qr, local, zks, zkr, zvs, zvr, hks, hkr, hvs, hvr,
+    ks, kr, vs, vr, qs, qr, local, zks, zkr, zvs, zvr, hks, hkr, hvs, hvr, zws, zwr,
     rs, rr, fs, fr, lsem, lrem, psem, prem, wsem, wrem, tsem, trem,
 ):
     nt = nz * ny
@@ -79,24 +80,51 @@
         return pl.ds(pl.multiple_of(ROW + b * BAND, ROW), BAND)
 
     own_k = pltpu.make_async_copy(k_ref.at[0, :, chunk(y)], kpad.at[band_rows(y)], local.at[0])
-    own_v = pltpu.make_async_copy(v_ref.at[0, :, chunk(y)], vpad.at[band_rows(y)], local.at[1])
+    own_v = pltpu.make_async_copy(v_ref.at[0, :, chunk(y)], vbuf.at[y], local.at[1])
     own_q = pltpu.make_async_copy(q_ref.at[0, :, chunk(y)], qbuf.at[y], local.at[2])
     own_k.start()
     own_v.start()
     own_q.start()
 
+    small = [
+        pltpu.make_async_copy(gid_hbm, gid_ref, local.at[4]),
+        pltpu.make_async_copy(qg_hbm, qg_ref, local.at[5]),
+        pltpu.make_async_copy(kg_hbm, kg_ref, local.at[6]),
+    ]
+    for c in small:
+        c.start()
+
+    chip = f // 2
+    mirror_t = (nz - 1 - z) * ny + y
+
+    def wrap(i, n):
+        return jnp.where(i >= n, i - n, i)
+
+    def t_dev(p):
+        return (f, p)
+
+    def f_dev(p):
+        return (p, jnp.where((p // 2) % 2 == chip % 2, t, mirror_t))
+
     barrier = pltpu.get_barrier_semaphore()
 
-    def greet_t(d, carry):
-        pl.semaphore_signal(barrier, inc=1, device_id=(f, (t + d) % nt), device_id_type=MESH)
+    def greet(dev):
+        pl.semaphore_signal(barrier, inc=1, device_id=dev, device_id_type=MESH)
+
+    for d in range(1, ny):
+        greet((f, z * ny + wrap(y + d, ny)))
+
+    def greet_t(i, carry):
+        far_z = wrap(z + i // ny, nz)
+        greet((f, far_z * ny + i % ny))
         return carry
 
     def greet_f(d, carry):
-        pl.semaphore_signal(barrier, inc=1, device_id=((f + d) % nf, t), device_id_type=MESH)
+        greet(f_dev(wrap(f + d, nf)))
         return carry
 
-    lax.fori_loop(1, nt, greet_t, 0)
     lax.fori_loop(1, nf, greet_f, 0)
+    lax.fori_loop(ny, nt, greet_t, 0)
     pl.semaphore_wait(barrier, nt - 1 + nf - 1)
 
     order = [0]
@@ -114,7 +142,7 @@
 
     def v_copy(d):
         p = (y + d) % ny
-        return copy(v_ref.at[0, :, chunk(p)], vpad.at[band_rows(y)], vs.at[d], vr.at[d], y_dev(d))
+        return copy(v_ref.at[0, :, chunk(p)], vbuf.at[y], vs.at[d], vr.at[d], y_dev(d))
 
     def q_copy(d):
         p = (y + d) % ny
@@ -125,28 +153,37 @@
         k_copy(d).start()
 
     mine = pl.ds(pl.multiple_of(core * shard, 64), shard)
-    has_rows = f // 2 == y
-
-    def r_copy(d):
-        return copy(r_ref, rraw.at[mine], rs.at[d], rr.at[0], ((f + 2 * d) % nf, t))
+    holder = chip == y
+    relay = (chip // 2 == y // 2) & (chip != y)
+    leaf = chip // 2 != y // 2
+    lines = range(1, nf // 4)
+
+    def x_copy(src, d):
+        return copy(src, rraw.at[mine], rs.at[d], rr.at[0], ((f + 4 * d) % nf, t))
+
+    def mirror_copy():
+        return copy(r_ref, rraw.at[mine], rs.at[0], rr.at[0], f_dev(f + 2 - 4 * (chip % 2)))
 
     def r_local():
         return pltpu.make_async_copy(r_ref, rraw.at[mine], local.at[3])
 
-    @pl.when(has_rows)
+    @pl.when(holder)
     def _():
-        for d in range(1, nf // 2):
-            r_copy(d).start()
+        mirror_copy().start()
+        for d in lines:
+            x_copy(r_ref, d).start()
         r_local().start()
 
     for d in far_first:
         k_copy(d).wait_send()
     for d in far_first:
-        v_copy(d).start()
+        q_copy(d).start()
 
     own_k.wait()
     for d in far_first:
         k_copy(d).wait_recv()
+    for c in small:
+        c.wait()
     gid = gid_ref[0]
     gid_y, gid_z = lax.rem(gid, ny), lax.div(gid, ny)
 
@@ -157,24 +194,27 @@
             out = part if out is None else out + part
         return out.astype(BF16)
 
-    def pick_row(pad):
-        return pick([pad[ROW + b * BAND : ROW + (b + 1) * BAND, :] for b in range(ny)], gid_y)
-
     def z_dev(d):
         return (f, ((z + d) % nz) * ny + y)
 
     def z_copy(buf, ssem, rsem, d):
         return copy(buf.at[z], buf.at[z], ssem.at[d], rsem.at[d], z_dev(d))
 
-    def end_copies(pad, ssem, rsem):
-        up = copy(pad.at[pl.ds(rows, ROW)], pad.at[pl.ds(0, ROW)], ssem.at[0], rsem.at[0], z_dev(1))
-        down = copy(pad.at[pl.ds(ROW, ROW)], pad.at[pl.ds(ROW + rows, ROW)], ssem.at[1], rsem.at[1], z_dev(nz - 1))
+    def k_ends():
+        up = copy(kpad.at[pl.ds(rows, ROW)], kpad.at[pl.ds(0, ROW)], hks.at[0], hkr.at[0], z_dev(1))
+        down = copy(kpad.at[pl.ds(ROW, ROW)], kpad.at[pl.ds(ROW + rows, ROW)], hks.at[1], hkr.at[1], z_dev(nz - 1))
         return up, down
 
-    zk[z] = pick_row(kpad)
+    def v_ends():
+        low, high = pl.ds(0, ROW), pl.ds(ROW, ROW)
+        up = copy(vbuf.at[ny - 1, high], vend.at[low], hvs.at[0], hvr.at[0], z_dev(1))
+        down = copy(vbuf.at[0, low], vend.at[high], hvs.at[1], hvr.at[1], z_dev(nz - 1))
+        return up, down
+
+    zk[z] = pick([kpad[ROW + b * BAND : ROW + (b + 1) * BAND, :] for b in range(ny)], gid_y)
     for d in range(1, nz):
         z_copy(zk, zks, zkr, d).start()
-    for c in end_copies(kpad, hks, hkr):
+    for c in k_ends():
         c.start()
 
     q_gain = [qg_ref[pl.ds(y * hc + h, 1), :] for h in range(hc)]
@@ -193,13 +233,13 @@
     lax.fori_loop(0, ny, norm_band, 0)
 
     for d in far_first:
-        v_copy(d).wait_send()
-    for d in far_first:
-        q_copy(d).start()
+        q_copy(d).wait_send()
+    for d in far_first:
+        v_copy(d).start()
 
     for d in range(1, nz):
         z_copy(zk, zks, zkr, d).wait_recv()
-    for c in end_copies(kpad, hks, hkr):
+    for c in k_ends():
         c.wait_recv()
     norm_rows(pl.ds(0, ROW), ROW)
     norm_rows(pl.ds(ROW + rows, ROW), ROW)
@@ -207,27 +247,11 @@
     for h in range(hc):
         kng[h, :, :HEAD] = normalize(kg_raw[:, h * HEAD : (h + 1) * HEAD], k_gain[h])
 
-    own_v.wait()
-    for d in far_first:
-        v_copy(d).wait_recv()
-    zv[z] = pick_row(vpad)
-    for d in range(1, nz):
-        z_copy(zv, zvs, zvr, d).start()
-    for c in end_copies(vpad, hvs, hvr):
-        c.start()
-
-    @pl.when(has_rows)
+    @pl.when(relay)
     def _():
-        r_local().wait()
-
-    @pl.when(jnp.logical_not(has_rows))
-    def _():
-        r_copy(1).wait_recv()
-
-    def twin_copy(at):
-        return copy(rraw.at[at], rraw.at[at], fs, fr, (f + 1 - 2 * core, t))
-
-    twin_copy(mine).start()
+        mirror_copy().wait_recv()
+        for d in lines:
+            x_copy(rraw.at[mine], d).start()
 
     ones16 = jnp.ones((16, BAND), BF16)
     lane = lax.broadcasted_iota(jnp.int32, (BAND, WIN), 1)
@@ -261,17 +285,9 @@
             q_copy(ny - d).wait_recv()
         band((y + d) % ny)
 
-    for d in range(1, nz):
-        z_copy(zv, zvs, zvr, d).wait_recv()
-    for c in end_copies(vpad, hvs, hvr):
-        c.wait_recv()
-    other = pl.ds(pl.multiple_of((1 - core) * shard, 64), shard)
-    twin_copy(other).wait_recv()
-    rpad[:, CLASSES // HEAD * HEAD :] = jnp.zeros((width, PAD - CLASSES // HEAD * HEAD), BF16)
-    rpad[:, :CLASSES] = rraw[...]
-
-    vg = pick([zv[i] for i in range(nz)], gid_z)
-    pooled = []
+    half = lax.broadcasted_iota(jnp.int32, (1, HEAD), 1) < ROW
+    given = []
+    zw[z] = jnp.zeros((8, HEAD), F32)
     for h in range(hc):
         parts = [jnp.zeros((1, HEAD), F32) for _ in range(ny + 1)]
         far = jnp.zeros((1, HEAD), F32)
@@ -279,57 +295,26 @@
             parts[b] = parts[b] + w_s[b, h, 0:1, :HEAD]
             parts[b + 1] = parts[b + 1] + w_s[b, h, 0:1, HEAD:WIN]
             far = far + w_s[b, h, 0:1, WIN:]
-        cols = slice(h * HEAD, (h + 1) * HEAD)
-        pooled.append(row_dot(jnp.concatenate(parts, 1), vpad[:, cols], NN) + row_dot(far, vg[:, cols], NN))
-    pooled = jnp.concatenate(pooled, 1) * (1.0 / tokens)
-    logits = row_dot(pooled, rpad[...], NN)
-    for i in range(8):
-        lbuf[t, i : i + 1, :] = logits[:, i * HEAD : (i + 1) * HEAD]
-
-    def exchange(buf, n, me, dev, ssem, rsem):
-        def one(d):
-            return copy(buf.at[me], buf.at[me], ssem.at[d], rsem.at[d], dev((me + d) % n))
-
-        def start():
-            def step(d, carry):
-                one(d).start()
-                return carry
-
-            lax.fori_loop(1, n, step, 0)
-
-        def wait():
-            def step(d, carry):
-                one(d).wait_recv()
-                return carry
-
-            lax.fori_loop(1, n, step, 0)
-
-        def wait_sent():
-            def step(d, carry):
-                one(d).wait_send()
-                return carry
-
-            lax.fori_loop(1, n, step, 0)
-
-        return start, wait, wait_sent
-
-    def t_dev(p):
-        return (f, p)
-
-    def f_dev(p):
-        return (p, t)
-
-    def total_of(buf, n):
-        out = buf[0]
-        for i in range(1, n):
-            out = out + buf[i]
-        return out
-
-    l_start, l_wait, l_sent = exchange(lbuf, nt, t, t_dev, lsem, lrem)
-    p_start, p_wait, p_sent = exchange(pbuf, nf, f, f_dev, psem, prem)
-    w_start, w_wait, w_sent = exchange(wbuf, nf, f, f_dev, wsem, wrem)
-    t_start, t_wait, t_sent = exchange(tbuf, nt, t, t_dev, tsem, trem)
-    l_start()
+        given.append(parts)
+        zw[z, h : h + 1, :] = far
+        zw[z, hc + h : hc + h + 1, :] = jnp.where(half, parts[0], parts[ny])
+    for d in range(1, nz):
+        z_copy(zw, zws, zwr, d).start()
+
+    @pl.when(holder)
+    def _():
+        r_local().wait()
+
+    if nf > 4:
+
+        @pl.when(leaf)
+        def _():
+            mirror_copy().wait_recv()
+
+    def twin_copy(at):
+        return copy(rraw.at[at], rraw.at[at], fs, fr, (f + 1 - 2 * core, t))
+
+    twin_copy(mine).start()
 
     e_acc[...] = jnp.zeros_like(e_acc)
     eg_acc[...] = jnp.zeros_like(eg_acc)
@@ -355,7 +340,91 @@
             eg_acc[h] += kg[:, :HEAD].astype(F32) * got[:, :HEAD] - got[:, HEAD : 2 * HEAD] - got[:, 2 * HEAD :]
         return carry
 
-    lax.fori_loop(0, ny // 2, pulled, 0)
+    def pull_bands(first, last):
+        lax.fori_loop(min(first, ny), min(last, ny), pulled, 0)
+
+    pull_bands(0, 2)
+
+    other = pl.ds(pl.multiple_of((1 - core) * shard, 64), shard)
+    twin_copy(other).wait_recv()
+    rpad[:, CLASSES // HEAD * HEAD :] = jnp.zeros((width, PAD - CLASSES // HEAD * HEAD), BF16)
+    rpad[:, :CLASSES] = rraw[...]
+
+    for d in range(1, nz):
+        z_copy(zw, zws, zwr, d).wait_recv()
+    below = zw[lax.rem(z + nz - 1, nz)]
+    above = zw[lax.rem(z + 1, nz)]
+    all_far = zw[0]
+    for i in range(1, nz):
+        all_far = all_far + zw[i]
+    weights = []
+    for h in range(hc):
+        parts = given[h]
+        parts[0] = parts[0] + below[hc + h : hc + h + 1]
+        parts[ny] = parts[ny] + above[hc + h : hc + h + 1]
+        own = []
+        for b in range(ny):
+            tile = jnp.concatenate([parts[b][:, ROW:], parts[b + 1][:, :ROW]], 1)
+            own.append(tile + all_far[h : h + 1] * jnp.where(gid == z * ny + b, 1.0, 0.0))
+        weights.append(split3(jnp.concatenate(own, 1)))
+
+    def v_head(h):
+        return vbuf[:, :, h * HEAD : (h + 1) * HEAD].reshape(rows, HEAD)
+
+    own_v.wait()
+    for d in far_first:
+        v_copy(d).wait_recv()
+    pooled = [jnp.sum(dot(weights[h], v_head(h), NN), 0, keepdims=True) for h in range(hc)]
+    pooled = jnp.concatenate(pooled, 1) * (1.0 / tokens)
+    logits = row_dot(pooled, rpad[...], NN)
+    for i in range(8):
+        lbuf[t, i : i + 1, :] = logits[:, i * HEAD : (i + 1) * HEAD]
+
+    def exchange(buf, n, me, dev, ssem, rsem):
+        def one(d):
+            return copy(buf.at[me], buf.at[me], ssem.at[d], rsem.at[d], dev(jnp.where(me + d >= n, me + d - n, me + d)))
+
+        def start():
+            def step(d, carry):
+                one(d).start()
+                return carry
+
+            lax.fori_loop(1, n, step, 0)
+
+        def wait():
+            def step(d, carry):
+                one(d).wait_recv()
+                return carry
+
+            lax.fori_loop(1, n, step, 0)
+
+        def wait_sent():
+            def step(d, carry):
+                one(d).wait_send()
+                return carry
+
+            lax.fori_loop(1, n, step, 0)
+
+        return start, wait, wait_sent
+
+    def total_of(buf, n):
+        out = buf[0]
+        for i in range(1, n):
+            out = out + buf[i]
+        return out
+
+    l_start, l_wait, l_sent = exchange(lbuf, nt, t, t_dev, lsem, lrem)
+    p_start, p_wait, p_sent = exchange(pbuf, nf, f, f_dev, psem, prem)
+    w_start, w_wait, w_sent = exchange(wbuf, nf, f, f_dev, wsem, wrem)
+    t_start, t_wait, t_sent = exchange(tbuf, nt, t, t_dev, tsem, trem)
+    l_start()
+
+    for c in v_ends():
+        c.start()
+    zv[z] = pick([vbuf[b] for b in range(ny)], gid_y)
+    for d in range(1, nz):
+        z_copy(zv, zvs, zvr, d).start()
+    pull_bands(2, 5)
 
     l_wait()
     logits = total_of(lbuf, nt)
@@ -372,15 +441,33 @@
     pbuf[f] = probs
     p_start()
 
-    lax.fori_loop(ny // 2, ny, pulled, 0)
+    pull_bands(5, ny)
+    for d in range(1, nz):
+        z_copy(zv, zvs, zvr, d).wait_recv()
+    for c in v_ends():
+        c.wait_recv()
+    vg = pick([zv[i] for i in range(nz)], gid_z)
     e_bf[...] = e_acc[...].astype(BF16)
-    eg_bf[...] = eg_acc[...].astype(BF16)
+    ones_rows = jnp.ones((16, rows), BF16)
+    for h in range(hc):
+        cols = slice(h * HEAD, (h + 1) * HEAD)
+        eg = eg_acc[h].astype(BF16)
+        v = v_head(h)
+        m = dot(v, e_bf[h, ROW : ROW + rows, :], TN) + dot(vg[:, cols], eg, TN)
+        m = m + dot(vend[:ROW, cols], e_bf[h, :ROW, :], TN)
+        m = m + dot(vend[ROW:, cols], e_bf[h, ROW + rows :, :], TN)
+        middle = dot(v, ones_rows, (((0,), (1,)), ((), ())))[:, :1] * (1.0 / rows)
+        total = jnp.sum(e_bf[h].astype(F32), 0, keepdims=True) + jnp.sum(eg.astype(F32), 0, keepdims=True)
+        m = m - middle * total
+        high = m.astype(BF16)
+        pull[h, :, :HEAD] = high
+        pull[h, :, HEAD:] = (m - high.astype(F32)).astype(BF16)
 
     p_wait()
     mean = total_of(pbuf, nf) * (1.0 / nf)
     log_mean = jnp.where(valid, jnp.log(mean), 0.0)
     entropy = -all_sum(jnp.where(valid, mean * log_mean, 0.0))
-    ent_ref[...] = jnp.broadcast_to(entropy, ent_ref.shape)
+    ent_ref[...] = entropy
     upstream = jnp.where(valid, -(log_mean + 1.0) * (1.0 / nf), 0.0)
     dlogits = probs * (upstream - all_sum(probs * upstream))
     dlogits = jnp.concatenate([dlogits[i : i + 1] for i in range(8)], 1)
@@ -388,35 +475,40 @@
     wbuf[f] = jnp.zeros((8, HEAD), F32)
     for h in range(hc):
         cols = slice(h * HEAD, (h + 1) * HEAD)
-        down = dpooled[:, cols]
-        near = row_dot(down, vpad[:, cols], NT)
-        far = row_dot(down, vg[:, cols], NT)
-        middle = (jnp.sum(near, 1, keepdims=True) + jnp.sum(far, 1, keepdims=True)) * (1.0 / (rows + 2 * ROW + BAND))
-        got = row_dot(near - middle, e_bf[h], NN) + row_dot(far - middle, eg_bf[h], NN)
-        wbuf[f, h : h + 1, :] = got * SCALE
+        got = row_dot(dpooled[:, cols], pull[h], NN)
+        wbuf[f, h : h + 1, :] = (got[:, :HEAD] + got[:, HEAD:]) * SCALE
     w_start()
     w_wait()
     tbuf[t] = total_of(wbuf, nf)
     t_start()
     t_wait()
     for i in range(ny):
-        got = tbuf[i]
-        for j in range(1, nz):
-            got = got + tbuf[j * ny + i]
+        got = None
+        for j in range(nz):
+            row = jnp.where(chip % 2 == 0, j, nz - 1 - j)
+            part = tbuf[row * ny + i]
+            got = part if got is None else got + part
         w_out[i * hc : (i + 1) * hc, :] = got[:hc]
 
     for d in far_first:
-        q_copy(d).wait_send()
+        v_copy(d).wait_send()
     for d in range(1, nz):
         z_copy(zk, zks, zkr, d).wait_send()
         z_copy(zv, zvs, zvr, d).wait_send()
-    for c in end_copies(kpad, hks, hkr) + end_copies(vpad, hvs, hvr):
+        z_copy(zw, zws, zwr, d).wait_send()
+    for c in k_ends() + v_ends():
         c.wait_send()
 
-    @pl.when(has_rows)
+    @pl.when(holder)
     def _():
-        for d in range(1, nf // 2):
-            r_copy(d).wait_send()
+        mirror_copy().wait_send()
+        for d in lines:
+            x_copy(r_ref, d).wait_send()
+
+    @pl.when(relay)
+    def _():
+        for d in lines:
+            x_copy(rraw.at[mine], d).wait_send()
 
     twin_copy(mine).wait_send()
     l_sent()
@@ -438,13 +530,18 @@
         dma = pltpu.SemaphoreType.DMA
         vmem = pltpu.VMEM
         scratch = [
+            pltpu.SMEM((1,), jnp.int32),
+            vmem((heads, HEAD), F32),
+            vmem((heads, HEAD), F32),
             vmem((padded, width), BF16),
-            vmem((padded, width), BF16),
+            vmem((ny, BAND, width), BF16),
+            vmem((2 * ROW, width), BF16),
             vmem((ny, BAND, width), BF16),
             vmem((hc, padded, 2 * HEAD), BF16),
             vmem((hc, BAND, 2 * HEAD), BF16),
             vmem((nz, BAND, width), BF16),
             vmem((nz, BAND, width), BF16),
+            vmem((nz, 8, HEAD), F32),
             vmem((width, CLASSES), BF16),
             vmem((width, PAD), BF16),
             vmem((ny, hc, BAND, SEEN), BF16),
@@ -453,24 +550,24 @@
             vmem((hc, padded, HEAD), F32),
             vmem((hc, BAND, HEAD), F32),
             vmem((hc, padded, HEAD), BF16),
-            vmem((hc, BAND, HEAD), BF16),
+            vmem((hc, HEAD, 2 * HEAD), BF16),
             vmem((nt, 8, HEAD), F32),
             vmem((nf, 8, HEAD), F32),
             vmem((nf, 8, HEAD), F32),
             vmem((nt, 8, HEAD), F32),
         ]
-        scratch += [dma((ny,))] * 6 + [dma((4,))] + [dma((nz,))] * 4 + [dma((2,))] * 4
-        scratch += [dma((nf // 2,)), dma((1,)), dma, dma]
+        scratch += [dma((ny,))] * 6 + [dma((7,))] + [dma((nz,))] * 4 + [dma((2,))] * 4 + [dma((nz,))] * 2
+        scratch += [dma((nf // 4,)), dma((1,)), dma, dma]
         scratch += [dma((nt,))] * 2 + [dma((nf,))] * 4 + [dma((nt,))] * 2
         hbm = pl.BlockSpec(memory_space=pl.ANY)
         whole = pl.BlockSpec(memory_space=pltpu.VMEM)
         entropy, total = pl.pallas_call(
             functools.partial(kernel, ny, nz, nf, hc, tokens),
             out_shape=(
-                jax.ShapeDtypeStruct((8, HEAD), F32),
+                jax.ShapeDtypeStruct((1, 1), F32),
                 jax.ShapeDtypeStruct((heads, HEAD), F32),
             ),
-            in_specs=[pl.BlockSpec(memory_space=pltpu.SMEM), hbm, hbm, hbm, hbm, whole, whole],
+            in_specs=[hbm] * 7,
             out_specs=(whole, whole),
             scratch_shapes=scratch,
             compiler_params=pltpu.CompilerParams(
@@ -487,7 +584,7 @@
             k_gain.reshape(heads, HEAD),
         )
         total = total.reshape(-1)
-        return entropy[0, 0], total / q_gain, total / k_gain
+        return entropy.reshape(()), total / q_gain, total / k_gain
 
     return body
 

time: 144 us -> 107 us (0.74)
  Pallas kernels: 140 us -> 102 us
  between operations: 1.3 us -> 3.07 us
    pallas_call x1, Pallas kernels: 140 us -> 102 us  [body(): pl.pallas_call(functools.partial(kernel, ny, nz, nf, hc, tokens), out_sha...]
where the time goes in v2:
time: 107 us
  Pallas kernels  102 us (95%)
  between operations  3.07 us (3%)
  other arithmetic  1.32 us (1%)
    pallas_call x1, Pallas kernels, body(): pl.pallas_call(functools.partial(kernel, ny, nz, nf, hc, tokens), out_sha...  102 us

profile of v2, /device:TPU:1, one launch (start us, length us, event | category | flops | bytes accessed | tf_op | source)
XLA Modules:
  0.0 106.6 jit_solution(16978323345710320980)
XLA Ops:
  1.3 0.0 copy-start
  1.3 0.0 copy-start.1
  1.3 102.2 %adapt.1 = (f32[1,1]{1,0:T(1,128)}, f32[24,128]{1,0:T(8,128)}) custom-call(s32[1]{0:T(128)S(6)} %copy.11.gid_hbm, bf16[1,128,3072]{2,1,0:T(8,128)(2,1)} %q_ref.1, bf16[1,128,3072]{2,1,0:T(8,128)(2,1)} %k_ref.1, bf16[1,128,3072]{2,1,0:T(8,128)(2,1)} %v_ref.1, bf16[192,1000]{1,0:T(8,128)(2,1)} %r_ref.1, f32[24,128]{1,0:T(8,128)} %bitcast.6, f32[24,128]{1,0:T(8,128)} %bitcast.7), custom_call_target="tpu_custom_call" | custom-call | tf_op jit(solution)/shard_map/adapt/pallas_call | solution.py:564
  103.5 0.0 copy-done
  103.5 0.0 copy-done.1
  103.5 1.3 %bitcast_divide_fusion = (f32[3072]{0:T(1024)}, f32[3072]{0:T(1024)}) fusion(f32[3072]{0:T(1024)S(1)} %copy-done.1, f32[24,128]{1,0:T(8,128)} %get-tuple-element.6, f32[3072]{0:T(1024)S(1)} %copy-done), kind=kLoop, calls=%fused_computation | loop fusion | flops 6144 | bytes 61440 | tf_op jit(solution)/shard_map/div | solution.py:587
Async XLA Ops:
  1.3 102.2 %copy-start = (f32[3072]{0:T(1024)S(1)}, f32[3072]{0:T(1024)}, u32[]{:S(2)}) copy-start(f32[3072]{0:T(1024)} %param.12) | copy-start | bytes 36868
  1.3 102.2 %copy-start.1 = (f32[3072]{0:T(1024)S(1)}, f32[3072]{0:T(1024)}, u32[]{:S(2)}) copy-start(f32[3072]{0:T(1024)} %param.13) | copy-start | bytes 36868

commit v3 on v2

--- a/solution.py
+++ b/solution.py
@@ -100,31 +100,43 @@
     def wrap(i, n):
         return jnp.where(i >= n, i - n, i)
 
-    def t_dev(p):
-        return (f, p)
-
     def f_dev(p):
         return (p, jnp.where((p // 2) % 2 == chip % 2, t, mirror_t))
 
+    def t_peers(act):
+        def column(k, carry):
+            d = jnp.where(k % 2 == 1, ny // 2 - (k + 1) // 2, ny // 2 + k // 2)
+            far_y = wrap(y + d, ny)
+            for i in range(nz):
+                p = wrap(z + i, nz) * ny + far_y
+                act(p, (f, p), i * ny + d)
+            return carry
+
+        lax.fori_loop(0, ny - 1, column, 0)
+        for i in range(1, nz):
+            p = wrap(z + i, nz) * ny + y
+            act(p, (f, p), i * ny)
+
+    def f_peers(act):
+        nx = nf // 4
+        x = f // 4
+        steps = sorted(range(nf), key=lambda s: -(2 * min(s // 4, nx - s // 4) + 3 * (s // 2 % 2)))
+        for s in steps:
+            if s:
+                other = chip % 2
+                if s // 2 % 2:
+                    other = 1 - other
+                twin = 1 - core if s % 2 else core
+                p = (wrap(x + s // 4, nx) * 2 + other) * 2 + twin
+                act(p, f_dev(p), s)
+
     barrier = pltpu.get_barrier_semaphore()
 
     def greet(dev):
         pl.semaphore_signal(barrier, inc=1, device_id=dev, device_id_type=MESH)
 
-    for d in range(1, ny):
-        greet((f, z * ny + wrap(y + d, ny)))
-
-    def greet_t(i, carry):
-        far_z = wrap(z + i // ny, nz)
-        greet((f, far_z * ny + i % ny))
-        return carry
-
-    def greet_f(d, carry):
-        greet(f_dev(wrap(f + d, nf)))
-        return carry
-
-    lax.fori_loop(1, nf, greet_f, 0)
-    lax.fori_loop(ny, nt, greet_t, 0)
+    t_peers(lambda slot, dev, number: greet(dev))
+    f_peers(lambda slot, dev, number: greet(dev))
     pl.semaphore_wait(barrier, nt - 1 + nf - 1)
 
     order = [0]
@@ -343,7 +355,7 @@
     def pull_bands(first, last):
         lax.fori_loop(min(first, ny), min(last, ny), pulled, 0)
 
-    pull_bands(0, 2)
+    pull_bands(0, 4)
 
     other = pl.ds(pl.multiple_of((1 - core) * shard, 64), shard)
     twin_copy(other).wait_recv()
@@ -380,30 +392,21 @@
     for i in range(8):
         lbuf[t, i : i + 1, :] = logits[:, i * HEAD : (i + 1) * HEAD]
 
-    def exchange(buf, n, me, dev, ssem, rsem):
-        def one(d):
-            return copy(buf.at[me], buf.at[me], ssem.at[d], rsem.at[d], dev(jnp.where(me + d >= n, me + d - n, me + d)))
+    def exchange(buf, me, peers, ssem, rsem):
+        def out(dev, number):
+            return copy(buf.at[me], buf.at[me], ssem.at[number], rsem.at[me], dev)
+
+        def come(slot, dev):
+            return copy(buf.at[slot], buf.at[slot], ssem.at[0], rsem.at[slot], dev)
 
         def start():
-            def step(d, carry):
-                one(d).start()
-                return carry
-
-            lax.fori_loop(1, n, step, 0)
+            peers(lambda slot, dev, number: out(dev, number).start())
 
         def wait():
-            def step(d, carry):
-                one(d).wait_recv()
-                return carry
-
-            lax.fori_loop(1, n, step, 0)
+            peers(lambda slot, dev, number: come(slot, dev).wait_recv())
 
         def wait_sent():
-            def step(d, carry):
-                one(d).wait_send()
-                return carry
-
-            lax.fori_loop(1, n, step, 0)
+            peers(lambda slot, dev, number: out(dev, number).wait_send())
 
         return start, wait, wait_sent
 
@@ -413,10 +416,10 @@
             out = out + buf[i]
         return out
 
-    l_start, l_wait, l_sent = exchange(lbuf, nt, t, t_dev, lsem, lrem)
-    p_start, p_wait, p_sent = exchange(pbuf, nf, f, f_dev, psem, prem)
-    w_start, w_wait, w_sent = exchange(wbuf, nf, f, f_dev, wsem, wrem)
-    t_start, t_wait, t_sent = exchange(tbuf, nt, t, t_dev, tsem, trem)
+    l_start, l_wait, l_sent = exchange(lbuf, t, t_peers, lsem, lrem)
+    p_start, p_wait, p_sent = exchange(pbuf, f, f_peers, psem, prem)
+    w_start, w_wait, w_sent = exchange(wbuf, f, f_peers, wsem, wrem)
+    t_start, t_wait, t_sent = exchange(tbuf, t, t_peers, tsem, trem)
     l_start()
 
     for c in v_ends():
@@ -424,7 +427,7 @@
     zv[z] = pick([vbuf[b] for b in range(ny)], gid_y)
     for d in range(1, nz):
         z_copy(zv, zvs, zvr, d).start()
-    pull_bands(2, 5)
+    pull_bands(4, 7)
 
     l_wait()
     logits = total_of(lbuf, nt)
@@ -441,7 +444,7 @@
     pbuf[f] = probs
     p_start()
 
-    pull_bands(5, ny)
+    pull_bands(7, ny)
     for d in range(1, nz):
         z_copy(zv, zvs, zvr, d).wait_recv()
     for c in v_ends():
@@ -467,7 +470,7 @@
     mean = total_of(pbuf, nf) * (1.0 / nf)
     log_mean = jnp.where(valid, jnp.log(mean), 0.0)
     entropy = -all_sum(jnp.where(valid, mean * log_mean, 0.0))
-    ent_ref[...] = entropy
+    ent_ref[...] = jnp.broadcast_to(entropy, ent_ref.shape)
     upstream = jnp.where(valid, -(log_mean + 1.0) * (1.0 / nf), 0.0)
     dlogits = probs * (upstream - all_sum(probs * upstream))
     dlogits = jnp.concatenate([dlogits[i : i + 1] for i in range(8)], 1)
@@ -560,14 +563,15 @@
         scratch += [dma((nf // 4,)), dma((1,)), dma, dma]
         scratch += [dma((nt,))] * 2 + [dma((nf,))] * 4 + [dma((nt,))] * 2
         hbm = pl.BlockSpec(memory_space=pl.ANY)
+        in_hbm = pl.BlockSpec(memory_space=pltpu.HBM)
         whole = pl.BlockSpec(memory_space=pltpu.VMEM)
         entropy, total = pl.pallas_call(
             functools.partial(kernel, ny, nz, nf, hc, tokens),
             out_shape=(
-                jax.ShapeDtypeStruct((1, 1), F32),
+                jax.ShapeDtypeStruct((8, HEAD), F32),
                 jax.ShapeDtypeStruct((heads, HEAD), F32),
             ),
-            in_specs=[hbm] * 7,
+            in_specs=[in_hbm, hbm, hbm, hbm, hbm, in_hbm, in_hbm],
             out_specs=(whole, whole),
             scratch_shapes=scratch,
             compiler_params=pltpu.CompilerParams(
@@ -584,7 +588,7 @@
             k_gain.reshape(heads, HEAD),
         )
         total = total.reshape(-1)
-        return entropy.reshape(()), total / q_gain, total / k_gain
+        return entropy[0, 0], total / q_gain, total / k_gain
 
     return body
 

time: 107 us -> 107 us (level)
  between operations: 3.07 us -> 1.3 us
  local copies, waits for them, and re-layouts: 0.01 us -> 1.2 us
    slice x0 -> x1, local copies, waits for them, and re-layouts: none -> 1.19 us  [body(): return (entropy[0, 0], total / q_gain, total / k_gain)]
where the time goes in v3:
time: 107 us; the launch traced here: 106 us
  Pallas kernels  102 us (95%)
  other arithmetic  1.32 us (1%)
  between operations  1.3 us (1%)
  local copies, waits for them, and re-layouts  1.2 us (1%)
    pallas_call x1, Pallas kernels, body(): pl.pallas_call(functools.partial(kernel, ny, nz, nf, hc, tokens), out_sha...  102 us

profile of v3, /device:TPU:1, one launch (start us, length us, event | category | flops | bytes accessed | tf_op | source)
XLA Modules:
  0.0 106.3 jit_solution(6443885274378489191)
XLA Ops:
  1.3 0.0 copy-start
  1.3 0.0 copy-start.1
  1.3 102.5 %adapt.1 = (f32[8,128]{1,0:T(8,128)}, f32[24,128]{1,0:T(8,128)}) custom-call(s32[1]{0:T(128)S(6)} %copy.10.gid_hbm, bf16[1,128,3072]{2,1,0:T(8,128)(2,1)} %q_ref.1, bf16[1,128,3072]{2,1,0:T(8,128)(2,1)} %k_ref.1, bf16[1,128,3072]{2,1,0:T(8,128)(2,1)} %v_ref.1, bf16[192,1000]{1,0:T(8,128)(2,1)} %r_ref.1, f32[24,128]{1,0:T(8,128)} %bitcast.6, f32[24,128]{1,0:T(8,128)} %bitcast.7), custom_call_target="tpu_custom_call" | custom-call | tf_op jit(solution)/shard_map/adapt/pallas_call | solution.py:568
  103.8 1.2 %slice.3 = f32[1,1]{1,0:T(1,128)} slice(f32[8,128]{1,0:T(8,128)} %get-tuple-element.5), slice={[0:1], [0:1]} | slice | bytes 8 | tf_op jit(solution)/shard_map/slice | solution.py:591
  105.0 0.0 copy-done
  105.0 0.0 copy-done.1
  105.0 1.3 %bitcast_divide_fusion = (f32[3072]{0:T(1024)}, f32[3072]{0:T(1024)}) fusion(f32[3072]{0:T(1024)S(1)} %copy-done.1, f32[24,128]{1,0:T(8,128)} %get-tuple-element.6, f32[3072]{0:T(1024)S(1)} %copy-done), kind=kLoop, calls=%fused_computation | loop fusion | flops 6144 | bytes 61440 | tf_op jit(solution)/shard_map/div | solution.py:591
Async XLA Ops:
  1.3 103.7 %copy-start = (f32[3072]{0:T(1024)S(1)}, f32[3072]{0:T(1024)}, u32[]{:S(2)}) copy-start(f32[3072]{0:T(1024)} %param.12) | copy-start | bytes 36868
  1.3 103.7 %copy-start.1 = (f32[3072]{0:T(1024)S(1)}, f32[3072]{0:T(1024)}, u32[]{:S(2)}) copy-start(f32[3072]{0:T(1024)} %param.13) | copy-start | bytes 36868

commit v4 on v3

--- a/solution.py
+++ b/solution.py
@@ -103,8 +103,10 @@
     def f_dev(p):
         return (p, jnp.where((p // 2) % 2 == chip % 2, t, mirror_t))
 
-    def t_peers(act):
+    def t_peers(act, far_last=False):
         def column(k, carry):
+            if far_last:
+                k = ny - 2 - k
             d = jnp.where(k % 2 == 1, ny // 2 - (k + 1) // 2, ny // 2 + k // 2)
             far_y = wrap(y + d, ny)
             for i in range(nz):
@@ -112,23 +114,28 @@
                 act(p, (f, p), i * ny + d)
             return carry
 
+        def own_column():
+            for i in range(1, nz):
+                p = wrap(z + i, nz) * ny + y
+                act(p, (f, p), i * ny)
+
+        if far_last:
+            own_column()
         lax.fori_loop(0, ny - 1, column, 0)
-        for i in range(1, nz):
-            p = wrap(z + i, nz) * ny + y
-            act(p, (f, p), i * ny)
-
-    def f_peers(act):
+        if not far_last:
+            own_column()
+
+    def f_peers(act, far_last=False):
         nx = nf // 4
         x = f // 4
-        steps = sorted(range(nf), key=lambda s: -(2 * min(s // 4, nx - s // 4) + 3 * (s // 2 % 2)))
-        for s in steps:
-            if s:
-                other = chip % 2
-                if s // 2 % 2:
-                    other = 1 - other
-                twin = 1 - core if s % 2 else core
-                p = (wrap(x + s // 4, nx) * 2 + other) * 2 + twin
-                act(p, f_dev(p), s)
+        steps = sorted(range(1, nf), key=lambda s: -(2 * min(s // 4, nx - s // 4) + 3 * (s // 2 % 2)))
+        for s in steps[::-1] if far_last else steps:
+            other = chip % 2
+            if s // 2 % 2:
+                other = 1 - other
+            twin = 1 - core if s % 2 else core
+            p = (wrap(x + s // 4, nx) * 2 + other) * 2 + twin
+            act(p, f_dev(p), s)
 
     barrier = pltpu.get_barrier_semaphore()
 
@@ -403,10 +410,10 @@
             peers(lambda slot, dev, number: out(dev, number).start())
 
         def wait():
-            peers(lambda slot, dev, number: come(slot, dev).wait_recv())
+            peers(lambda slot, dev, number: come(slot, dev).wait_recv(), True)
 
         def wait_sent():
-            peers(lambda slot, dev, number: out(dev, number).wait_send())
+            peers(lambda slot, dev, number: out(dev, number).wait_send(), True)
 
         return start, wait, wait_sent
 
@@ -484,6 +491,32 @@
     w_wait()
     tbuf[t] = total_of(wbuf, nf)
     t_start()
+
+    for d in far_first:
+        v_copy(d).wait_send()
+    for d in range(1, nz):
+        z_copy(zk, zks, zkr, d).wait_send()
+        z_copy(zv, zvs, zvr, d).wait_send()
+        z_copy(zw, zws, zwr, d).wait_send()
+    for c in k_ends() + v_ends():
+        c.wait_send()
+
+    @pl.when(holder)
+    def _():
+        mirror_copy().wait_send()
+        for d in lines:
+            x_copy(r_ref, d).wait_send()
+
+    @pl.when(relay)
+    def _():
+        for d in lines:
+            x_copy(rraw.at[mine], d).wait_send()
+
+    twin_copy(mine).wait_send()
+    l_sent()
+    p_sent()
+    w_sent()
+    t_sent()
     t_wait()
     for i in range(ny):
         got = None
@@ -492,32 +525,6 @@
             part = tbuf[row * ny + i]
             got = part if got is None else got + part
         w_out[i * hc : (i + 1) * hc, :] = got[:hc]
-
-    for d in far_first:
-        v_copy(d).wait_send()
-    for d in range(1, nz):
-        z_copy(zk, zks, zkr, d).wait_send()
-        z_copy(zv, zvs, zvr, d).wait_send()
-        z_copy(zw, zws, zwr, d).wait_send()
-    for c in k_ends() + v_ends():
-        c.wait_send()
-
-    @pl.when(holder)
-    def _():
-        mirror_copy().wait_send()
-        for d in lines:
-            x_copy(r_ref, d).wait_send()
-
-    @pl.when(relay)
-    def _():
-        for d in lines:
-            x_copy(rraw.at[mine], d).wait_send()
-
-    twin_copy(mine).wait_send()
-    l_sent()
-    p_sent()
-    w_sent()
-    t_sent()
 
 
 def make_body(ny):

time: 107 us -> 106 us (level)
  no operation moved by 1% of the time
where the time goes in v4:
time: 106 us
  Pallas kernels  102 us (96%)
  other arithmetic  1.32 us (1%)
  between operations  1.3 us (1%)
  local copies, waits for them, and re-layouts  1.2 us (1%)
    pallas_call x1, Pallas kernels, body(): pl.pallas_call(functools.partial(kernel, ny, nz, nf, hc, tokens), out_sha...  102 us

profile of v4, /device:TPU:1, one launch (start us, length us, event | category | flops | bytes accessed | tf_op | source)
XLA Modules:
  0.0 105.9 jit_solution(11859116858932910647)
XLA Ops:
  1.3 0.0 copy-start
  1.3 0.0 copy-start.1
  1.3 102.1 %adapt.1 = (f32[8,128]{1,0:T(8,128)}, f32[24,128]{1,0:T(8,128)}) custom-call(s32[1]{0:T(128)S(6)} %copy.10.gid_hbm, bf16[1,128,3072]{2,1,0:T(8,128)(2,1)} %q_ref.1, bf16[1,128,3072]{2,1,0:T(8,128)(2,1)} %k_ref.1, bf16[1,128,3072]{2,1,0:T(8,128)(2,1)} %v_ref.1, bf16[192,1000]{1,0:T(8,128)(2,1)} %r_ref.1, f32[24,128]{1,0:T(8,128)} %bitcast.6, f32[24,128]{1,0:T(8,128)} %bitcast.7), custom_call_target="tpu_custom_call" | custom-call | tf_op jit(solution)/shard_map/adapt/pallas_call | solution.py:575
  103.4 1.2 %slice.3 = f32[1,1]{1,0:T(1,128)} slice(f32[8,128]{1,0:T(8,128)} %get-tuple-element.5), slice={[0:1], [0:1]} | slice | bytes 8 | tf_op jit(solution)/shard_map/slice | solution.py:598
  104.6 0.0 copy-done
  104.6 0.0 copy-done.1
  104.6 1.3 %bitcast_divide_fusion = (f32[3072]{0:T(1024)}, f32[3072]{0:T(1024)}) fusion(f32[3072]{0:T(1024)S(1)} %copy-done.1, f32[24,128]{1,0:T(8,128)} %get-tuple-element.6, f32[3072]{0:T(1024)S(1)} %copy-done), kind=kLoop, calls=%fused_computation | loop fusion | flops 6144 | bytes 61440 | tf_op jit(solution)/shard_map/div | solution.py:598
Async XLA Ops:
  1.3 103.3 %copy-start = (f32[3072]{0:T(1024)S(1)}, f32[3072]{0:T(1024)}, u32[]{:S(2)}) copy-start(f32[3072]{0:T(1024)} %param.12) | copy-start | bytes 36868
  1.3 103.3 %copy-start.1 = (f32[3072]{0:T(1024)S(1)}, f32[3072]{0:T(1024)}, u32[]{:S(2)}) copy-start(f32[3072]{0:T(1024)} %param.13) | copy-start | bytes 36868

commit v5 on v4

--- a/solution.py
+++ b/solution.py
@@ -167,8 +167,8 @@
         p = (y + d) % ny
         return copy(q_ref.at[0, :, chunk(p)], qbuf.at[y], qs.at[d], qr.at[d], y_dev(d))
 
-    far_first = order[:0:-1]
-    for d in far_first:
+    others = order[1:]
+    for d in others:
         k_copy(d).start()
 
     mine = pl.ds(pl.multiple_of(core * shard, 64), shard)
@@ -193,13 +193,13 @@
             x_copy(r_ref, d).start()
         r_local().start()
 
-    for d in far_first:
+    for d in others:
         k_copy(d).wait_send()
-    for d in far_first:
+    for d in others:
         q_copy(d).start()
 
     own_k.wait()
-    for d in far_first:
+    for d in others:
         k_copy(d).wait_recv()
     for c in small:
         c.wait()
@@ -251,9 +251,9 @@
 
     lax.fori_loop(0, ny, norm_band, 0)
 
-    for d in far_first:
+    for d in others:
         q_copy(d).wait_send()
-    for d in far_first:
+    for d in others:
         v_copy(d).start()
 
     for d in range(1, nz):
@@ -391,7 +391,7 @@
         return vbuf[:, :, h * HEAD : (h + 1) * HEAD].reshape(rows, HEAD)
 
     own_v.wait()
-    for d in far_first:
+    for d in others:
         v_copy(d).wait_recv()
     pooled = [jnp.sum(dot(weights[h], v_head(h), NN), 0, keepdims=True) for h in range(hc)]
     pooled = jnp.concatenate(pooled, 1) * (1.0 / tokens)
@@ -492,7 +492,7 @@
     tbuf[t] = total_of(wbuf, nf)
     t_start()
 
-    for d in far_first:
+    for d in others:
         v_copy(d).wait_send()
     for d in range(1, nz):
         z_copy(zk, zks, zkr, d).wait_send()

time: 106 us -> 104 us (0.981)
  Pallas kernels: 102 us -> 99.6 us
    pallas_call x1, Pallas kernels: 102 us -> 99.6 us  [body(): pl.pallas_call(functools.partial(kernel, ny, nz, nf, hc, tokens), out_sha...]
where the time goes in v5:
time: 104 us; the launch traced here: 103 us
  Pallas kernels  99.6 us (96%)
  other arithmetic  1.32 us (1%)
  between operations  1.3 us (1%)
  local copies, waits for them, and re-layouts  1.2 us (1%)
    pallas_call x1, Pallas kernels, body(): pl.pallas_call(functools.partial(kernel, ny, nz, nf, hc, tokens), out_sha...  99.6 us

profile of v5, /device:TPU:1, one launch (start us, length us, event | category | flops | bytes accessed | tf_op | source)
XLA Modules:
  0.0 103.5 jit_solution(3405690651467418787)
XLA Ops:
  1.3 0.0 copy-start
  1.3 0.0 copy-start.1
  1.3 99.6 %adapt.1 = (f32[8,128]{1,0:T(8,128)}, f32[24,128]{1,0:T(8,128)}) custom-call(s32[1]{0:T(128)S(6)} %copy.10.gid_hbm, bf16[1,128,3072]{2,1,0:T(8,128)(2,1)} %q_ref.1, bf16[1,128,3072]{2,1,0:T(8,128)(2,1)} %k_ref.1, bf16[1,128,3072]{2,1,0:T(8,128)(2,1)} %v_ref.1, bf16[192,1000]{1,0:T(8,128)(2,1)} %r_ref.1, f32[24,128]{1,0:T(8,128)} %bitcast.6, f32[24,128]{1,0:T(8,128)} %bitcast.7), custom_call_target="tpu_custom_call" | custom-call | tf_op jit(solution)/shard_map/adapt/pallas_call | solution.py:575
  100.9 1.2 %slice.3 = f32[1,1]{1,0:T(1,128)} slice(f32[8,128]{1,0:T(8,128)} %get-tuple-element.5), slice={[0:1], [0:1]} | slice | bytes 8 | tf_op jit(solution)/shard_map/slice | solution.py:598
  102.1 0.0 copy-done
  102.1 0.0 copy-done.1
  102.1 1.3 %bitcast_divide_fusion = (f32[3072]{0:T(1024)}, f32[3072]{0:T(1024)}) fusion(f32[3072]{0:T(1024)S(1)} %copy-done.1, f32[24,128]{1,0:T(8,128)} %get-tuple-element.6, f32[3072]{0:T(1024)S(1)} %copy-done), kind=kLoop, calls=%fused_computation | loop fusion | flops 6144 | bytes 61440 | tf_op jit(solution)/shard_map/div | solution.py:598
Async XLA Ops:
  1.3 100.9 %copy-start = (f32[3072]{0:T(1024)S(1)}, f32[3072]{0:T(1024)}, u32[]{:S(2)}) copy-start(f32[3072]{0:T(1024)} %param.12) | copy-start | bytes 36868
  1.3 100.8 %copy-start.1 = (f32[3072]{0:T(1024)S(1)}, f32[3072]{0:T(1024)}, u32[]{:S(2)}) copy-start(f32[3072]{0:T(1024)} %param.13) | copy-start | bytes 36868

commit v6 on v5

--- a/solution.py
+++ b/solution.py
@@ -170,6 +170,10 @@
     others = order[1:]
     for d in others:
         k_copy(d).start()
+    for d in others:
+        q_copy(d).start()
+    for d in others:
+        v_copy(d).start()
 
     mine = pl.ds(pl.multiple_of(core * shard, 64), shard)
     holder = chip == y
@@ -193,10 +197,6 @@
             x_copy(r_ref, d).start()
         r_local().start()
 
-    for d in others:
-        k_copy(d).wait_send()
-    for d in others:
-        q_copy(d).start()
 
     own_k.wait()
     for d in others:
@@ -251,10 +251,6 @@
 
     lax.fori_loop(0, ny, norm_band, 0)
 
-    for d in others:
-        q_copy(d).wait_send()
-    for d in others:
-        v_copy(d).start()
 
     for d in range(1, nz):
         z_copy(zk, zks, zkr, d).wait_recv()
@@ -493,6 +489,8 @@
     t_start()
 
     for d in others:
+        k_copy(d).wait_send()
+        q_copy(d).wait_send()
         v_copy(d).wait_send()
     for d in range(1, nz):
         z_copy(zk, zks, zkr, d).wait_send()

time: 104 us -> 104 us (level)
  no operation moved by 1% of the time
where the time goes in v6:
time: 104 us
  Pallas kernels  100 us (96%)
  other arithmetic  1.32 us (1%)
  between operations  1.3 us (1%)
  local copies, waits for them, and re-layouts  1.2 us (1%)
    pallas_call x1, Pallas kernels, body(): pl.pallas_call(functools.partial(kernel, ny, nz, nf, hc, tokens), out_sha...  100 us

profile of v6, /device:TPU:1, one launch (start us, length us, event | category | flops | bytes accessed | tf_op | source)
XLA Modules:
  0.0 104.0 jit_solution(1711083876768710031)
XLA Ops:
  1.3 0.0 copy-start
  1.3 0.0 copy-start.1
  1.3 100.2 %adapt.1 = (f32[8,128]{1,0:T(8,128)}, f32[24,128]{1,0:T(8,128)}) custom-call(s32[1]{0:T(128)S(6)} %copy.10.gid_hbm, bf16[1,128,3072]{2,1,0:T(8,128)(2,1)} %q_ref.1, bf16[1,128,3072]{2,1,0:T(8,128)(2,1)} %k_ref.1, bf16[1,128,3072]{2,1,0:T(8,128)(2,1)} %v_ref.1, bf16[192,1000]{1,0:T(8,128)(2,1)} %r_ref.1, f32[24,128]{1,0:T(8,128)} %bitcast.6, f32[24,128]{1,0:T(8,128)} %bitcast.7), custom_call_target="tpu_custom_call" | custom-call | tf_op jit(solution)/shard_map/adapt/pallas_call | solution.py:573
  101.5 1.2 %slice.3 = f32[1,1]{1,0:T(1,128)} slice(f32[8,128]{1,0:T(8,128)} %get-tuple-element.5), slice={[0:1], [0:1]} | slice | bytes 8 | tf_op jit(solution)/shard_map/slice | solution.py:596
  102.6 0.0 copy-done
  102.7 0.0 copy-done.1
  102.7 1.3 %bitcast_divide_fusion = (f32[3072]{0:T(1024)}, f32[3072]{0:T(1024)}) fusion(f32[3072]{0:T(1024)S(1)} %copy-done.1, f32[24,128]{1,0:T(8,128)} %get-tuple-element.6, f32[3072]{0:T(1024)S(1)} %copy-done), kind=kLoop, calls=%fused_computation | loop fusion | flops 6144 | bytes 61440 | tf_op jit(solution)/shard_map/div | solution.py:596
Async XLA Ops:
  1.3 101.4 %copy-start = (f32[3072]{0:T(1024)S(1)}, f32[3072]{0:T(1024)}, u32[]{:S(2)}) copy-start(f32[3072]{0:T(1024)} %param.12) | copy-start | bytes 36868
  1.3 101.4 %copy-start.1 = (f32[3072]{0:T(1024)S(1)}, f32[3072]{0:T(1024)}, u32[]{:S(2)}) copy-start(f32[3072]{0:T(1024)} %param.13) | copy-start | bytes 36868
